TPU v7x, 512 devices: a whole 4x8x8 slice. The times are simulated.
512 devices in a mesh: tile: 64 (over x, z, y_lo), orient: 8 (over y_hi, core).
Axes of the slice: x: 4, y: 8 (y_hi: 4, y_lo: 2; y = y_hi * 2 + y_lo), z: 8, core: 2. Of those that a mesh axis runs over, the one named last changes fastest.
Arguments:
- micrographs: bfloat16 [64, 512, 512], P('tile'), may hold values from -6 to 6
- templates: bfloat16 [64, 8, 256, 256], P('tile', 'orient'), may hold values from -0.0234375 to 0.0234375
- quarter_turns: int32 [64, 8], P('tile', 'orient'), may hold values from 0 to 3
- plan: int32 [64], replicated, may hold values from 0 to 63, each once
Outputs:
- best_score: float32 [64, 512, 512], P('tile', 'orient')
- mean_score: float32 [64, 512, 512], P('tile', 'orient')
Inputs may be any that keep to these rules, and one draw needn't show every extreme that they name: `plan`: every tile index appears exactly once; the steps use the first 2 entries.
All inputs are finite; a program needn't handle non-finite values.
Results may differ from a plain program's by a relative error of at most 0.018.
Values may be sent and summed in bfloat16 or wider, within the bound.
A program may use at most 64 MiB of HBM per device.

v0:
```python
import jax
import jax.numpy as jnp
from jax import lax
from jax.sharding import PartitionSpec as P

STEPS = 2


def broadcast(block, axis, source):
    block = jnp.where(lax.axis_index(axis) == source, block, jnp.zeros_like(block))
    return lax.psum(block, axis)


def dft_tables(length):
    positions = jnp.arange(length, dtype=jnp.int32)
    phase_index = positions[:, None] * positions[None, :] % length
    angles = 2.0 * jnp.pi / length * phase_index.astype(jnp.float32)
    return (jnp.cos(angles).astype(jnp.bfloat16), jnp.sin(angles).astype(jnp.bfloat16))


def forward_spectra(pixels, cosine_table, sine_table):
    length = cosine_table.shape[0]
    extent = pixels.shape[-1]
    left_stack = jnp.concatenate([cosine_table[:, :extent], sine_table[:, :extent]], axis=0)
    right_stack = jnp.concatenate([cosine_table[:extent, :], sine_table[:extent, :]], axis=1)
    stacked = jnp.einsum("kn,bnm->bkm", left_stack, pixels, preferred_element_type=jnp.float32)
    part_re = stacked[:, :length].astype(jnp.bfloat16)
    part_im = (-stacked[:, length:]).astype(jnp.bfloat16)
    from_re = jnp.einsum("bkn,nm->bkm", part_re, right_stack, preferred_element_type=jnp.float32)
    from_im = jnp.einsum("bkn,nm->bkm", part_im, right_stack, preferred_element_type=jnp.float32)
    spec_re = (from_re[..., :length] + from_im[..., length:]).astype(jnp.bfloat16)
    spec_im = (from_im[..., :length] - from_re[..., length:]).astype(jnp.bfloat16)
    return (spec_re, spec_im)


def rotate(pixels, quarter):
    options = [pixels, jnp.rot90(pixels, 1), jnp.rot90(pixels, 2), jnp.rot90(pixels, 3)]
    result = options[0]
    for turn_count in range(1, 4):
        result = jnp.where(quarter == turn_count, options[turn_count], result)
    return result


def template_spectra(pixels, quarters, cosine_table, sine_table):
    rotated = jax.vmap(rotate)(pixels, quarters)
    return forward_spectra(rotated, cosine_table, sine_table)


def correlate(spec_re, spec_im, tmpl_re, tmpl_im, cosine_table, sine_table):
    length = cosine_table.shape[0]
    right_stack = jnp.concatenate([cosine_table, sine_table], axis=1)
    inverse_left = jnp.concatenate([cosine_table, -sine_table], axis=1)
    x_re = spec_re.astype(jnp.float32)
    x_im = spec_im.astype(jnp.float32)
    t_re = tmpl_re.astype(jnp.float32)[None]
    t_im = tmpl_im.astype(jnp.float32)[None]
    prod_re = (x_re * t_re + x_im * t_im).astype(jnp.bfloat16)
    prod_im = (x_im * t_re - x_re * t_im).astype(jnp.bfloat16)
    from_re = jnp.einsum("tkn,nm->tkm", prod_re, right_stack, preferred_element_type=jnp.float32)
    from_im = jnp.einsum("tkn,nm->tkm", prod_im, right_stack, preferred_element_type=jnp.float32)
    mid_re = (from_re[..., :length] - from_im[..., length:]).astype(jnp.bfloat16)
    mid_im = (from_re[..., length:] + from_im[..., :length]).astype(jnp.bfloat16)
    joined = jnp.concatenate([mid_re, mid_im], axis=1)
    scores = jnp.einsum("kn,tnm->tkm", inverse_left, joined, preferred_element_type=jnp.float32)
    return scores / float(length * length)


def per_device(micrographs, templates, quarter_turns, plan):
    length = micrographs.shape[-1]
    cosine_table, sine_table = dft_tables(length)
    spec_re, spec_im = forward_spectra(micrographs, cosine_table, sine_table)
    best_score = jnp.full(micrographs.shape, -jnp.inf, dtype=jnp.float32)
    running_sum = jnp.zeros(micrographs.shape, jnp.float32)
    block_count = templates.shape[1]
    for step_index in range(STEPS):
        owner_index = plan[step_index]
        got_pixels, got_quarters = (
            broadcast(templates[0], "tile", owner_index),
            broadcast(quarter_turns[0], "tile", owner_index),
        )
        tmpl_re, tmpl_im = template_spectra(got_pixels, got_quarters, cosine_table, sine_table)
        scores = correlate(spec_re, spec_im, tmpl_re[0], tmpl_im[0], cosine_table, sine_table)
        best_score = jnp.maximum(best_score, scores)
        running_sum = running_sum + scores
    groups = lax.axis_size("orient")
    best_score = lax.pmax(best_score.astype(jnp.bfloat16), "orient").astype(best_score.dtype)
    running_sum = lax.psum(running_sum.astype(jnp.bfloat16), "orient").astype(jnp.float32)
    row_share = length // groups
    row_start = lax.axis_index("orient") * row_share
    best_score = lax.dynamic_slice_in_dim(best_score, row_start, row_share, 1)
    running_sum = lax.dynamic_slice_in_dim(running_sum, row_start, row_share, 1)
    mean_score = running_sum / float(STEPS * block_count * groups)
    return (best_score, mean_score)


def solution(mesh):
    in_specs = (P("tile", None, None), P("tile", "orient", None, None), P("tile", "orient"), P())
    out_specs = (P("tile", "orient", None), P("tile", "orient", None))
    return jax.shard_map(
        per_device, mesh=mesh, in_specs=in_specs, out_specs=out_specs, check_vma=False
    )
```

profile of v0, /device:TPU:1, one launch (start us, length us, event | category | flops | bytes accessed | tf_op | source)
XLA Modules:
  0.0 765.5 jit_solution(1561606788596092640)
XLA Ops:
  7.2 1.3 fusion.77
  9.8 1.6 select_bitcast_fusion
  11.5 4.3 sine_convert_fusion
  17.4 2.0 convolution_bitcast_fusion.4
  19.4 2.0 convolution_bitcast_fusion.5
  21.4 4.6 fusion.57
  26.7 26.2 %all-reduce = (s32[1]{0:T(128)}, s32[1]{0:T(128)}) all-reduce(s32[1]{0:T(128)S(6)} %select_n.100, s32[1]{0:T(128)S(6)} %select_n.108), channel_id=1, replica_groups=mesh['tile'=64,'orient'=8] {'tile'}, use_global_device_ids=true, to_apply=%region_0.1 | all-reduce | flops 2 | bytes 16 | tf_op jit(solution)/shard_map/psum | solution.py:11
  56.7 2.5 fusion.18
  59.2 484.7 %all-reduce.10.cloned.1.call-done = (bf16[1,256,256]{2,1,0:T(8,128)(2,1)}, bf16[1,256,256]{2,1,0:T(8,128)(2,1)}) async-done(((bf16[1,256,256]{2,1,0:T(8,128)(2,1)}, bf16[1,256,256]{2,1,0:T(8,128)(2,1)}), (bf16[1,256,256]{2,1,0:T(8,128)(2,1)}, bf16[1,256,256]{2,1,0:T(8,128)(2,1)})) %all-reduce.10.cloned.1.call-update) | async-done | bytes 262160 | tf_op jit(solution)/shard_map/psum | solution.py:11
  543.9 1.0 copy.8
  544.9 2.9 rev.30
  547.9 1.3 rev.31
  549.2 1.5 rev.29
  550.7 1.5 convolution_bitcast_fusion.11
  553.7 2.1 convolution_bitcast_fusion.1
  555.8 2.1 convolution_bitcast_fusion
  558.6 1.5 rev.27
  560.2 2.8 rev.28
  562.9 2.9 rev.26
  565.8 1.4 convolution_bitcast_fusion.12
  577.0 99.0 %all-reduce.8.cloned.1.call-done = bf16[1,512,512]{1,2,0:T(8,128)(2,1)} async-done(((bf16[1,512,512]{1,2,0:T(8,128)(2,1)}), bf16[1,512,512]{1,2,0:T(8,128)(2,1)}) %all-reduce.8.cloned.1.call-update) | async-done | bytes 524304 | tf_op jit(solution)/shard_map/psum | solution.py:87
  676.1 1.0 convert_multiply_fusion.8
  677.8 79.4 %all-reduce.6.cloned.1.call-done = bf16[1,512,512]{1,2,0:T(8,128)(2,1)} async-done(((bf16[1,512,512]{1,2,0:T(8,128)(2,1)}), bf16[1,512,512]{1,2,0:T(8,128)(2,1)}) %all-reduce.6.cloned.1.call-update) | async-done | bytes 524304 | tf_op jit(solution)/shard_map/pmax | solution.py:86
  757.2 1.0 dynamic-slice_convert_fusion
  (38 shorter events, 15.1 us)
Async XLA Ops:
  7.2 9.5 %copy-start = (bf16[1,512,512]{2,1,0:T(8,128)(2,1)S(1)}, bf16[1,512,512]{2,1,0:T(8,128)(2,1)}, u32[]{:S(2)}) copy-start(bf16[1,512,512]{2,1,0:T(8,128)(2,1)} %param.4) | copy-start | bytes 1572868
  7.2 536.8 %all-reduce.10.cloned.1.call-start = ((), (), s32[]{:S(2)}) async-start(), calls=%async_computation.2 | async-start | bytes 524288 | tf_op jit(solution)/shard_map/psum | solution.py:11
  11.5 664.6 %all-reduce.8.cloned.1.call-start = ((), (), s32[]{:S(2)}) async-start(), calls=%async_computation.1 | async-start | bytes 1048576 | tf_op jit(solution)/shard_map/psum | solution.py:87
  555.8 2.1 copy-start.3
  569.6 1.6 copy-start.1
  569.6 2.2 copy-start.2
  572.4 1.0 copy-start.4
  575.9 181.3 %all-reduce.6.cloned.1.call-start = ((), (), s32[]{:S(2)}) async-start(), calls=%async_computation | async-start | bytes 1048576 | tf_op jit(solution)/shard_map/pmax | solution.py:86
Sparse Core Ops, SparseCore 0:
  11.6 532.2 all-reduce.9
  576.1 99.9 all-reduce.7
  679.0 78.1 all-reduce.5
where the time goes:
time: 767 us; the launch traced here: 766 us
  waiting for transfers between devices  663 us (86%)
  blocking collectives  26.2 us (3%)
  local copies, waits for them, and re-layouts  20.3 us (3%)
  between operations  19.6 us (3%)
  other arithmetic  19.4 us (3%)
  matrix products  16.7 us (2%)
    psum x1, waiting for transfers between devices, broadcast(): return lax.psum(block, axis)  485 us
    psum x1, waiting for transfers between devices, per_device(): lax.psum(running_sum.astype(jnp.bfloat16), 'orient').astype(jnp.float32)  99 us
    pmax x1, waiting for transfers between devices, per_device(): lax.pmax(best_score.astype(jnp.bfloat16), 'orient').astype(best_score.dtype)  79.4 us
    psum x1, blocking collectives, broadcast(): return lax.psum(block, axis)  26.2 us
  transfers between devices with their start and end apart: 3, of which 3 were waited for; matrix products, arithmetic and copies ran while one was open for 3% of the time, Pallas kernels for 0%

commit v1 on v0

v1 whole, which is shorter than its diff:
```python
import functools

import jax
import jax.numpy as jnp
import numpy as np
from jax import lax
from jax.experimental import pallas as pl
from jax.experimental.pallas import tpu as pltpu
from jax.sharding import PartitionSpec as P

MESH = pl.DeviceIdType.MESH
BF = jnp.bfloat16
F32 = jnp.float32
SIDE = 512
SEARCHED = 16


def radix_tables():
    j = np.arange(128)
    forward = []
    for r in range(4):
        phase = (np.outer(4 * j + r, j) % SIDE).astype(np.float32)
        angle = np.float32(2.0 * np.pi / SIDE) * phase
        c, s = np.cos(angle), np.sin(angle)
        forward.append(np.block([[c, s], [-s, c]]))
    forward = np.stack(forward).astype(np.float32)
    return forward.astype(jnp.bfloat16), forward.transpose(0, 2, 1).astype(jnp.bfloat16)


def coords():
    tile = lax.axis_index("tile")
    orient = lax.axis_index("orient")
    x, z = lax.div(tile, 16), lax.rem(lax.div(tile, 2), 8)
    y = lax.div(orient, 2) * 2 + lax.rem(tile, 2)
    return x, z, y, lax.rem(orient, 2)


def device(x, z, y, core):
    return (x * 16 + z * 2 + lax.rem(y, 2), lax.div(y, 2) * 2 + core)


def remote(src, dst, send, recv, target):
    return pltpu.make_async_remote_copy(
        src_ref=src, dst_ref=dst, send_sem=send, recv_sem=recv, device_id=target, device_id_type=MESH
    )


def dot(a, b):
    return jnp.dot(a, b, preferred_element_type=F32)


def rotate(block, quarter):
    turns = jnp.full((256, 256), quarter, jnp.int32)
    row = lax.broadcasted_iota(jnp.int32, (256, 256), 0)
    col = lax.broadcasted_iota(jnp.int32, (256, 256), 1)
    same = (row == col).astype(F32)
    swapped = (row + col == 255).astype(F32)
    flip_rows = jnp.where((turns == 1) | (turns == 2), swapped, same).astype(BF)
    flip_cols = jnp.where((turns == 2) | (turns == 3), swapped, same).astype(BF)
    wide = block.astype(F32)
    turned = jnp.where((turns == 1) | (turns == 3), wide.T, wide).astype(BF)
    return dot(dot(flip_rows, turned).astype(BF), flip_cols).astype(BF)


def tile_spectrum(mic, fwd, fwd_t, work, spec):
    quarters = [mic[0, 128 * q : 128 * q + 128, :].astype(F32) for q in range(4)]
    a, b = quarters[0] + quarters[2], quarters[1] + quarters[3]
    c, d = quarters[0] - quarters[2], quarters[1] - quarters[3]
    outs = [
        dot(fwd[0, :, :128], (a + b).astype(BF)),
        dot(fwd[1], jnp.concatenate([c, -d], axis=0).astype(BF)),
        dot(fwd[2, :, :128], (a - b).astype(BF)),
        dot(fwd[3], jnp.concatenate([c, d], axis=0).astype(BF)),
    ]
    for r1 in range(4):
        re = [outs[r1][:128, 128 * p : 128 * p + 128] for p in range(4)]
        im = [outs[r1][128:, 128 * p : 128 * p + 128] for p in range(4)]
        rows = pl.ds(128 * r1, 128)
        rs, rd, im_s, im_d = re[0] + re[2], re[0] - re[2], im[0] + im[2], im[0] - im[2]
        ro, rp, io, ip = re[1] + re[3], re[1] - re[3], im[1] + im[3], im[1] - im[3]
        pairs = [(rs + ro, im_s + io), (rd + ip, im_d - rp), (rs - ro, im_s - io), (rd - ip, im_d + rp)]
        for r2, (p_re, p_im) in enumerate(pairs):
            work[r2, rows, :128] = p_re.astype(BF)
            work[r2, rows, 128:] = p_im.astype(BF)
    for r2 in range(4):
        spec[r2] = dot(work[r2], fwd_t[r2]).astype(BF)


def inverse_rows(fwd_t, quarter, left):
    for r in range(4):
        turn = lax.rem(quarter * r, 4)
        turn = jnp.full((128, 128), turn, jnp.int32)
        c = fwd_t[r, :128, :128].astype(F32)
        s = fwd_t[r, 128:, :128].astype(F32)
        new_c = jnp.where(turn == 0, c, jnp.where(turn == 1, -s, jnp.where(turn == 2, -c, s))).astype(BF)
        new_s = jnp.where(turn == 0, s, jnp.where(turn == 1, c, jnp.where(turn == 2, -s, -c)))
        left[:128, 256 * r : 256 * r + 128] = new_c
        left[128:, 256 * r + 128 : 256 * r + 256] = new_c
        left[:128, 256 * r + 128 : 256 * r + 256] = (-new_s).astype(BF)
        left[128:, 256 * r : 256 * r + 128] = new_s.astype(BF)


def pair_scores(block, fwd, fwd_t, spec, left, work, prod, best, total, first):
    a0, a1 = [jnp.concatenate([block(q, 0, 0), block(q, 1, 0)], axis=1).astype(F32) for q in range(2)]
    b0, b1 = [jnp.concatenate([block(q, 0, 1), block(q, 1, 1)], axis=1).astype(F32) for q in range(2)]
    stacked = [(a0 + a1, b0 + b1), (a0 + b1, b0 - a1), (a0 - a1, b0 - b1), (a0 - b1, b0 + a1)]
    for r1 in range(4):
        out = dot(fwd[r1], jnp.concatenate(stacked[r1], axis=0).astype(BF))
        re0, re1, im0, im1 = out[:128, :128], out[:128, 128:], out[128:, :128], out[128:, 128:]
        rows = pl.ds(128 * r1, 128)
        pairs = [(re0 + re1, im0 + im1), (re0 + im1, im0 - re1), (re0 - re1, im0 - im1), (re0 - im1, im0 + re1)]
        for r2, (p_re, p_im) in enumerate(pairs):
            work[r2, rows, :128] = p_re.astype(BF)
            work[r2, rows, 128:] = p_im.astype(BF)
    for r2 in range(4):
        found = dot(work[r2], fwd_t[r2])
        t_re, t_im = found[:, :128].astype(BF).astype(F32), found[:, 128:].astype(BF).astype(F32)
        x_re, x_im = spec[r2, :, :128].astype(F32), spec[r2, :, 128:].astype(F32)
        p_re = (x_re * t_re + x_im * t_im).astype(BF)
        p_im = (x_im * t_re - x_re * t_im).astype(BF)
        lanes = pl.ds(128 * r2, 128)
        for r1 in range(4):
            prod[pl.ds(256 * r1, 128), lanes] = p_re[128 * r1 : 128 * r1 + 128]
            prod[pl.ds(256 * r1 + 128, 128), lanes] = p_im[128 * r1 : 128 * r1 + 128]
    mid = dot(left[...], prod[...]).astype(BF)
    u = []
    for r2 in range(4):
        lanes = slice(128 * r2, 128 * r2 + 128)
        u.append(dot(jnp.concatenate([mid[:128, lanes], mid[128:, lanes]], axis=1), fwd[r2]))
    re = [v[:, :128] for v in u]
    im = [v[:, 128:] for v in u]
    rs, rd, im_s, im_d = re[0] + re[2], re[0] - re[2], im[0] + im[2], im[0] - im[2]
    ro, rp, io, ip = re[1] + re[3], re[1] - re[3], im[1] + im[3], im[1] - im[3]
    one = [rs + ro, rd - ip, rs - ro, rd + ip]
    two = [-(im_s + io), -(im_d + rp), io - im_s, rp - im_d]
    for q in range(4):
        lanes = pl.ds(128 * q, 128)
        top, both = jnp.maximum(one[q], two[q]), one[q] + two[q]
        if first:
            best[:, lanes] = top
            total[:, lanes] = both
        else:
            best[:, lanes] = jnp.maximum(best[:, lanes], top)
            total[:, lanes] = total[:, lanes] + both


def kernel(
    quarter, plan, mic, tmpl, fwd, fwd_t, best_out, mean_out,
    turned, got, line, tx, tz, spec, work, prod, left, best, total, give, take,
    a_send, a_recv, y_send, y_recv, sx_send, sx_recv, sz_send, sz_recv, bx_send, bx_recv, bz_send, bz_recv, c_send, c_recv,
):
    x, z, y, core = coords()
    around = [(dx, dz) for dx in range(4) for dz in range(8) if (dx, dz) != (0, 0)]
    plane = [(lax.rem(x + dx, 4), lax.rem(z + dz, 8)) for dx, dz in around]
    x_peers = [device(lax.rem(x + d, 4), z, y, core) for d in range(1, 4)]
    z_peers = [device(x, lax.rem(z + d, 8), y, core) for d in range(1, 8)]
    y_peers = [device(x, z, lax.rem(y + d, 8), core) for d in range(1, 8)]
    other = device(x, z, y, 1 - core)

    barrier = pltpu.get_barrier_semaphore()
    greeted = [device(px, pz, y, core) for px, pz in plane] + y_peers + [other]
    for target in greeted:
        pl.semaphore_signal(barrier, inc=1, device_id=target, device_id_type=MESH)

    block = rotate(tmpl[0, 0], quarter[0, 0])
    for q in range(2):
        for h in range(2):
            turned[pl.ds(16 * q + 8 * h, 8)] = block[128 * q : 128 * q + 128, 128 * h : 128 * h + 128].reshape(8, 16, 128)
    tile_spectrum(mic, fwd, fwd_t, work, spec)
    inverse_rows(fwd_t, lax.div(y, 2), left)
    pl.semaphore_wait(barrier, len(greeted))

    mine = x * 8 + z
    sends = []
    for i, (px, pz) in enumerate(plane):
        copy = remote(turned.at[px * 8 + pz], got.at[mine], a_send.at[i], a_recv.at[i], device(px, pz, y, core))
        copy.start()
        sends.append(copy)
    got[mine] = turned[mine]
    for copy in sends:
        copy.wait_recv()

    owners = [plan[s] for s in range(2)]
    for s in range(2):
        line[y, s] = got[lax.div(owners[s], 2)]
    y_copies = []
    for i, target in enumerate(y_peers):
        copy = remote(line.at[y], line.at[y], y_send.at[i], y_recv.at[i], target)
        copy.start()
        y_copies.append(copy)
    for copy in y_copies:
        copy.wait_recv()
    sends += y_copies

    for s in range(2):
        low = lax.rem(owners[s], 2)
        tz[z, x, s] = line[low, s]
        for p in range(3):
            tx[x, p, z, s] = line[2 * (p + 1) + low, s]
    z_copies = [
        remote(tx.at[x, :, z], tx.at[x, :, z], sz_send.at[i], sz_recv.at[i], target) for i, target in enumerate(z_peers)
    ]
    x_copies = [
        remote(tz.at[z, x], tz.at[z, x], sx_send.at[i], sx_recv.at[i], target) for i, target in enumerate(x_peers)
    ]
    for copy in z_copies + x_copies:
        copy.start()
    for copy in x_copies:
        copy.wait_recv()
    last_z = [remote(tz.at[z], tz.at[z], bz_send.at[i], bz_recv.at[i], target) for i, target in enumerate(z_peers)]
    for copy in last_z:
        copy.start()
    for copy in z_copies:
        copy.wait_recv()
    last_x = []
    for p in range(3):
        group = []
        for i, target in enumerate(x_peers):
            copy = remote(tx.at[x, p], tx.at[x, p], bx_send.at[p, i], bx_recv.at[p, i], target)
            copy.start()
            group.append(copy)
        last_x.append(group)
    sends += z_copies + x_copies + last_z

    def from_x(p):
        return lambda q, h, s: tx[2 * q + h, p, :, s].reshape(128, 128)

    def from_z(q, h, s):
        return tz[:, 2 * q + h, s].reshape(128, 128)

    for copy in last_x[0]:
        copy.wait_recv()
    pair_scores(from_x(0), fwd, fwd_t, spec, left, work, prod, best, total, True)
    for copy in last_z:
        copy.wait_recv()
    pair_scores(from_z, fwd, fwd_t, spec, left, work, prod, best, total, False)
    for p in range(1, 3):
        for copy in last_x[p]:
            copy.wait_recv()
        pair_scores(from_x(p), fwd, fwd_t, spec, left, work, prod, best, total, False)

    scale = 1.0 / (SIDE * SIDE)
    theirs, ours = pl.ds((1 - core) * 64, 64), pl.ds(core * 64, 64)
    give[0] = (best[theirs, :] * scale).astype(BF)
    give[1] = (total[theirs, :] * scale).astype(BF)
    swap = remote(give, take, c_send, c_recv, other)
    swap.start()
    swap.wait_recv()
    best_out[0] = jnp.maximum(best[ours, :] * scale, take[0].astype(F32))
    mean_out[0] = (total[ours, :] * scale + take[1].astype(F32)) * (1.0 / SEARCHED)
    swap.wait_send()
    for copy in sends:
        copy.wait_send()
    for group in last_x:
        for copy in group:
            copy.wait_send()


def per_device(micrographs, templates, quarter_turns, plan):
    fwd, fwd_t = radix_tables()
    vmem, smem = pl.BlockSpec(memory_space=pltpu.VMEM), pl.BlockSpec(memory_space=pltpu.SMEM)
    dma = pltpu.SemaphoreType.DMA
    out = jax.ShapeDtypeStruct((1, 64, SIDE), F32)
    return pl.pallas_call(
        kernel,
        out_shape=(out, out),
        in_specs=[smem, smem, vmem, vmem, vmem, vmem],
        out_specs=(vmem, vmem),
        scratch_shapes=[
            pltpu.VMEM((32, 16, 128), BF),
            pltpu.VMEM((32, 16, 128), BF),
            pltpu.VMEM((8, 2, 16, 128), BF),
            pltpu.VMEM((4, 3, 8, 2, 16, 128), BF),
            pltpu.VMEM((8, 4, 2, 16, 128), BF),
            pltpu.VMEM((4, 512, 256), BF),
            pltpu.VMEM((4, 512, 256), BF),
            pltpu.VMEM((1024, 512), BF),
            pltpu.VMEM((256, 1024), BF),
            pltpu.VMEM((128, 512), F32),
            pltpu.VMEM((128, 512), F32),
            pltpu.VMEM((2, 64, 512), BF),
            pltpu.VMEM((2, 64, 512), BF),
            dma((31,)), dma((31,)), dma((7,)), dma((7,)), dma((3,)), dma((3,)), dma((7,)), dma((7,)),
            dma((3, 3)), dma((3, 3)), dma((7,)), dma((7,)), dma(()), dma(()),
        ],
        compiler_params=pltpu.CompilerParams(collective_id=0, has_side_effects=True, vmem_limit_bytes=40 << 20),
        name="match",
    )(quarter_turns, plan, micrographs, templates, jnp.asarray(fwd), jnp.asarray(fwd_t))


def solution(mesh):
    in_specs = (P("tile", None, None), P("tile", "orient", None, None), P("tile", "orient"), P())
    out_specs = (P("tile", "orient", None), P("tile", "orient", None))
    return jax.shard_map(per_device, mesh=mesh, in_specs=in_specs, out_specs=out_specs, check_vma=False)
```

time: 767 us -> 58.4 us (0.08)
  waiting for transfers between devices: 663 us -> 0 us
  Pallas kernels: 0 us -> 51.4 us
  blocking collectives: 26.2 us -> 0 us
  other arithmetic: 19.4 us -> 0 us
  between operations: 19.6 us -> 1.32 us
  matrix products: 16.7 us -> 0 us
  local copies, waits for them, and re-layouts: 20.3 us -> 5.34 us
    psum x2 -> x0, waiting for transfers between devices: 584 us -> none  [the longest x1 485 us: broadcast(): return lax.psum(block, axis)]
    pmax x1 -> x0, waiting for transfers between devices: 79.4 us -> none  [per_device(): lax.pmax(best_score.astype(jnp.bfloat16), 'orient').astype(best_score.dtype)]
    pallas_call x0 -> x1, Pallas kernels: none -> 51.4 us  [per_device(): pl.pallas_call(kernel, out_shape=(out, out), in_specs=[smem, smem, vmem,...]
    psum x1 -> x0, blocking collectives: 26.2 us -> none  [broadcast(): return lax.psum(block, axis)]
    dot_general x15 -> x0, matrix products: 16.7 us -> none  [the longest x3 3.63 us: forward_spectra(): jnp.einsum('kn,bnm->bkm', left_stack, pixels, preferred_element_type=jnp....]
    rev x6 -> x0, local copies, waits for them, and re-layouts: 13 us -> none  [the longest x2 4.46 us: rotate(): jnp.rot90(pixels, 2)]
    convert_element_type x9 -> x0, other arithmetic: 12.1 us -> none  [the longest x1 4.31 us: dft_tables(): jnp.sin(angles).astype(jnp.bfloat16)]
  transfers between devices with their start and end apart: 3 -> 0, of which waited for: 3 -> 0; matrix products, arithmetic and copies ran while one was open for 3% -> 0% of each run, Pallas kernels for 0% -> 0%
where the time goes in v1:
time: 58.4 us; the launch traced here: 58.1 us
  Pallas kernels  51.4 us (88%)
  local copies, waits for them, and re-layouts  5.34 us (9%)
  between operations  1.32 us (2%)
    pallas_call x1, Pallas kernels, per_device(): pl.pallas_call(kernel, out_shape=(out, out), in_specs=[smem, smem, vmem,...  51.4 us
    unnamed x12, local copies, waits for them, and re-layouts  5.34 us

profile of v1, /device:TPU:1, one launch (start us, length us, event | category | flops | bytes accessed | tf_op | source)
XLA Modules:
  0.0 58.1 jit_solution(16681240249633842882)
XLA Ops:
  0.6 0.0 copy-start.4
  1.3 0.0 copy-done.4
  1.3 0.0 copy-start
  1.3 1.0 %copy-done = bf16[1,512,512]{2,1,0:T(8,128)(2,1)S(1)} copy-done((bf16[1,512,512]{2,1,0:T(8,128)(2,1)S(1)}, bf16[1,512,512]{2,1,0:T(8,128)(2,1)}, u32[]{:S(2)}) %copy-start) | copy-done | bytes 524312
  2.4 0.0 copy-start.1
  2.4 1.0 %copy-done.1 = bf16[4,256,256]{2,1,0:T(8,128)(2,1)S(1)} copy-done((bf16[4,256,256]{2,1,0:T(8,128)(2,1)S(1)}, bf16[4,256,256]{2,1,0:T(8,128)(2,1)}, u32[]{:S(2)}) %copy-start.1) | copy-done | bytes 524312
  3.4 0.0 copy-start.2
  3.4 1.0 %copy-done.2 = bf16[4,256,256]{2,1,0:T(8,128)(2,1)S(1)} copy-done((bf16[4,256,256]{2,1,0:T(8,128)(2,1)S(1)}, bf16[4,256,256]{2,1,0:T(8,128)(2,1)}, u32[]{:S(2)}) %copy-start.2) | copy-done | bytes 524312
  4.4 0.0 copy-start.3
  4.4 0.9 %copy-done.3 = bf16[1,1,256,256]{3,2,1,0:T(8,128)(2,1)S(1)} copy-done((bf16[1,1,256,256]{3,2,1,0:T(8,128)(2,1)S(1)}, bf16[1,1,256,256]{3,2,1,0:T(8,128)(2,1)}, u32[]{:S(2)}) %copy-start.3) | copy-done | bytes 131096
  5.3 51.4 %match.1 = (f32[1,64,512]{2,1,0:T(8,128)S(1)}, f32[1,64,512]{2,1,0:T(8,128)S(1)}) custom-call(s32[1,1]{1,0:T(1,128)S(6)} %copy.10.quarter, s32[64]{0:T(128)S(1)} %copy-done.4, bf16[1,512,512]{2,1,0:T(8,128)(2,1)S(1)} %copy-done, bf16[1,1,256,256]{3,2,1,0:T(8,128)(2,1)S(1)} %copy-done.3, bf16[4,256,256]{2,1,0:T(8,128)(2,1)S(1)} %copy-done.2, ...), custom_call_target="tpu_custom_call" | custom-call | tf_op jit(solution)/shard_map/match/pallas_call | solution.py:264
  56.8 0.7 %copy.11 = f32[1,64,512]{2,1,0:T(8,128)} copy(f32[1,64,512]{2,1,0:T(8,128)S(1)} %get-tuple-element.4) | data formatting | bytes 262144
  57.4 0.7 %copy.12 = f32[1,64,512]{2,1,0:T(8,128)} copy(f32[1,64,512]{2,1,0:T(8,128)S(1)} %get-tuple-element.5) | data formatting | bytes 262144
Async XLA Ops:
  0.6 0.7 %copy-start.4 = (s32[64]{0:T(128)S(1)}, s32[64]{0:T(128)}, u32[]{:S(2)}) copy-start(s32[64]{0:T(128)} %plan.1) | copy-start | bytes 772
  1.3 1.0 %copy-start = (bf16[1,512,512]{2,1,0:T(8,128)(2,1)S(1)}, bf16[1,512,512]{2,1,0:T(8,128)(2,1)}, u32[]{:S(2)}) copy-start(bf16[1,512,512]{2,1,0:T(8,128)(2,1)} %mic.1) | copy-start | bytes 1572868
  2.4 1.0 %copy-start.1 = (bf16[4,256,256]{2,1,0:T(8,128)(2,1)S(1)}, bf16[4,256,256]{2,1,0:T(8,128)(2,1)}, u32[]{:S(2)}) copy-start(bf16[4,256,256]{2,1,0:T(8,128)(2,1)} %constant.5.clone.fwd_t) | copy-start | bytes 1572868
  3.4 1.0 %copy-start.2 = (bf16[4,256,256]{2,1,0:T(8,128)(2,1)S(1)}, bf16[4,256,256]{2,1,0:T(8,128)(2,1)}, u32[]{:S(2)}) copy-start(bf16[4,256,256]{2,1,0:T(8,128)(2,1)} %constant.4.clone.fwd) | copy-start | bytes 1572868
  4.4 0.9 %copy-start.3 = (bf16[1,1,256,256]{3,2,1,0:T(8,128)(2,1)S(1)}, bf16[1,1,256,256]{3,2,1,0:T(8,128)(2,1)}, u32[]{:S(2)}) copy-start(bf16[1,1,256,256]{3,2,1,0:T(8,128)(2,1)} %tmpl.1) | copy-start | bytes 393220

commit v2 on v1

--- a/solution.py
+++ b/solution.py
@@ -145,29 +145,43 @@
 
 
 def kernel(
-    quarter, plan, mic, tmpl, fwd, fwd_t, best_out, mean_out,
-    turned, got, line, tx, tz, spec, work, prod, left, best, total, give, take,
+    quarter_in, plan_in, mic_in, tmpl_in, fwd_in, fwd_t_in, out,
+    quarter, plan, mic, tmpl, fwd, fwd_t, load, turned, got, line, tx, tz, spec, work, prod, left, best, total, give, take,
     a_send, a_recv, y_send, y_recv, sx_send, sx_recv, sz_send, sz_recv, bx_send, bx_recv, bz_send, bz_recv, c_send, c_recv,
 ):
     x, z, y, core = coords()
+
+    def hops(dx, dz):
+        return min(dx, 4 - dx) + min(dz, 8 - dz)
+
     around = [(dx, dz) for dx in range(4) for dz in range(8) if (dx, dz) != (0, 0)]
+    around.sort(key=lambda step: -hops(*step))
     plane = [(lax.rem(x + dx, 4), lax.rem(z + dz, 8)) for dx, dz in around]
-    x_peers = [device(lax.rem(x + d, 4), z, y, core) for d in range(1, 4)]
-    z_peers = [device(x, lax.rem(z + d, 8), y, core) for d in range(1, 8)]
-    y_peers = [device(x, z, lax.rem(y + d, 8), core) for d in range(1, 8)]
+    x_peers = [device(lax.rem(x + d, 4), z, y, core) for d in (2, 1, 3)]
+    y_peers = [device(x, z, lax.rem(y + d, 8), core) for d in (4, 3, 5, 2, 6, 1, 7)]
+    z_others = [k + (z <= k).astype(jnp.int32) for k in range(7)]
+    z_peers = [device(x, other_z, y, core) for other_z in z_others]
     other = device(x, z, y, 1 - core)
 
     barrier = pltpu.get_barrier_semaphore()
     greeted = [device(px, pz, y, core) for px, pz in plane] + y_peers + [other]
+    loads = [
+        pltpu.make_async_copy(src, dst, load.at[i])
+        for i, (src, dst) in enumerate(
+            [(quarter_in, quarter), (tmpl_in, tmpl), (fwd_in, fwd), (mic_in, mic), (fwd_t_in, fwd_t), (plan_in, plan)]
+        )
+    ]
     for target in greeted:
         pl.semaphore_signal(barrier, inc=1, device_id=target, device_id_type=MESH)
+    for copy in loads:
+        copy.start()
+    loads[0].wait()
+    loads[1].wait()
 
     block = rotate(tmpl[0, 0], quarter[0, 0])
     for q in range(2):
         for h in range(2):
             turned[pl.ds(16 * q + 8 * h, 8)] = block[128 * q : 128 * q + 128, 128 * h : 128 * h + 128].reshape(8, 16, 128)
-    tile_spectrum(mic, fwd, fwd_t, work, spec)
-    inverse_rows(fwd_t, lax.div(y, 2), left)
     pl.semaphore_wait(barrier, len(greeted))
 
     mine = x * 8 + z
@@ -177,50 +191,67 @@
         copy.start()
         sends.append(copy)
     got[mine] = turned[mine]
+    for copy in loads[2:]:
+        copy.wait()
+    tile_spectrum(mic, fwd, fwd_t, work, spec)
+    inverse_rows(fwd_t, lax.div(y, 2), left)
     for copy in sends:
         copy.wait_recv()
 
     owners = [plan[s] for s in range(2)]
     for s in range(2):
         line[y, s] = got[lax.div(owners[s], 2)]
-    y_copies = []
     for i, target in enumerate(y_peers):
-        copy = remote(line.at[y], line.at[y], y_send.at[i], y_recv.at[i], target)
-        copy.start()
-        y_copies.append(copy)
-    for copy in y_copies:
-        copy.wait_recv()
-    sends += y_copies
-
-    for s in range(2):
-        low = lax.rem(owners[s], 2)
-        tz[z, x, s] = line[low, s]
-        for p in range(3):
-            tx[x, p, z, s] = line[2 * (p + 1) + low, s]
-    z_copies = [
-        remote(tx.at[x, :, z], tx.at[x, :, z], sz_send.at[i], sz_recv.at[i], target) for i, target in enumerate(z_peers)
-    ]
+        copy = remote(line.at[y], line.at[y], y_send.at[i], y_recv.at[y], target)
+        copy.start()
+        sends.append(copy)
+
+    odd = [jnp.full((16, 128), lax.rem(owners[s], 2), jnp.int32) for s in range(2)]
+
+    def arrived(pair):
+        for low in range(2):
+            source = 2 * pair + low
+
+            @pl.when(source != y)
+            def _():
+                remote(line.at[source], line.at[source], y_send.at[0], y_recv.at[source], other).wait_recv()
+
+        return [jnp.where(odd[s] == 0, line[2 * pair, s], line[2 * pair + 1, s]) for s in range(2)]
+
+    own = lax.div(y, 2)
+    for s, tile in enumerate(arrived(own)):
+        tz[z, x, s] = tile
     x_copies = [
         remote(tz.at[z, x], tz.at[z, x], sx_send.at[i], sx_recv.at[i], target) for i, target in enumerate(x_peers)
     ]
-    for copy in z_copies + x_copies:
-        copy.start()
+    for copy in x_copies:
+        copy.start()
+    for p, step in enumerate((1, 3, 2)):
+        for s, tile in enumerate(arrived(lax.rem(own + step, 4))):
+            tx[x, p, z, s] = tile
+        for i, target in enumerate(z_peers):
+            copy = remote(tx.at[x, p, z], tx.at[x, p, z], sz_send.at[p, i], sz_recv.at[p, z], target)
+            copy.start()
+            sends.append(copy)
     for copy in x_copies:
         copy.wait_recv()
-    last_z = [remote(tz.at[z], tz.at[z], bz_send.at[i], bz_recv.at[i], target) for i, target in enumerate(z_peers)]
-    for copy in last_z:
-        copy.start()
-    for copy in z_copies:
-        copy.wait_recv()
+    for i, target in enumerate(z_peers):
+        copy = remote(tz.at[z], tz.at[z], bz_send.at[i], bz_recv.at[z], target)
+        copy.start()
+        sends.append(copy)
     last_x = []
     for p in range(3):
-        group = []
-        for i, target in enumerate(x_peers):
-            copy = remote(tx.at[x, p], tx.at[x, p], bx_send.at[p, i], bx_recv.at[p, i], target)
+        for i, source in enumerate(z_others):
+            remote(tx.at[x, p, source], tx.at[x, p, source], sz_send.at[p, i], sz_recv.at[p, source], other).wait_recv()
+        group = [
+            remote(tx.at[x, p], tx.at[x, p], bx_send.at[p, i], bx_recv.at[p, i], target)
+            for i, target in enumerate(x_peers)
+        ]
+        for copy in group:
             copy.start()
-            group.append(copy)
         last_x.append(group)
-    sends += z_copies + x_copies + last_z
+        sends += group
+    sends += x_copies
 
     def from_x(p):
         return lambda q, h, s: tx[2 * q + h, p, :, s].reshape(128, 128)
@@ -231,42 +262,43 @@
     for copy in last_x[0]:
         copy.wait_recv()
     pair_scores(from_x(0), fwd, fwd_t, spec, left, work, prod, best, total, True)
-    for copy in last_z:
-        copy.wait_recv()
+    for i, source in enumerate(z_others):
+        remote(tz.at[source], tz.at[source], bz_send.at[i], bz_recv.at[source], other).wait_recv()
     pair_scores(from_z, fwd, fwd_t, spec, left, work, prod, best, total, False)
     for p in range(1, 3):
         for copy in last_x[p]:
             copy.wait_recv()
         pair_scores(from_x(p), fwd, fwd_t, spec, left, work, prod, best, total, False)
 
-    scale = 1.0 / (SIDE * SIDE)
     theirs, ours = pl.ds((1 - core) * 64, 64), pl.ds(core * 64, 64)
-    give[0] = (best[theirs, :] * scale).astype(BF)
-    give[1] = (total[theirs, :] * scale).astype(BF)
+    give[0] = best[theirs, :].astype(BF)
+    give[1] = total[theirs, :].astype(BF)
     swap = remote(give, take, c_send, c_recv, other)
     swap.start()
     swap.wait_recv()
-    best_out[0] = jnp.maximum(best[ours, :] * scale, take[0].astype(F32))
-    mean_out[0] = (total[ours, :] * scale + take[1].astype(F32)) * (1.0 / SEARCHED)
+    out[0] = jnp.maximum(best[ours, :], take[0].astype(F32))
+    out[1] = total[ours, :] + take[1].astype(F32)
     swap.wait_send()
     for copy in sends:
         copy.wait_send()
-    for group in last_x:
-        for copy in group:
-            copy.wait_send()
 
 
 def per_device(micrographs, templates, quarter_turns, plan):
     fwd, fwd_t = radix_tables()
-    vmem, smem = pl.BlockSpec(memory_space=pltpu.VMEM), pl.BlockSpec(memory_space=pltpu.SMEM)
     dma = pltpu.SemaphoreType.DMA
-    out = jax.ShapeDtypeStruct((1, 64, SIDE), F32)
-    return pl.pallas_call(
+    raw = pl.pallas_call(
         kernel,
-        out_shape=(out, out),
-        in_specs=[smem, smem, vmem, vmem, vmem, vmem],
-        out_specs=(vmem, vmem),
+        out_shape=jax.ShapeDtypeStruct((2, 64, SIDE), F32),
+        in_specs=[pl.BlockSpec(memory_space=pltpu.HBM)] * 6,
+        out_specs=pl.BlockSpec(memory_space=pltpu.VMEM),
         scratch_shapes=[
+            pltpu.SMEM((1, 1), jnp.int32),
+            pltpu.SMEM((64,), jnp.int32),
+            pltpu.VMEM((1, SIDE, SIDE), BF),
+            pltpu.VMEM((1, 1, 256, 256), BF),
+            pltpu.VMEM((4, 256, 256), BF),
+            pltpu.VMEM((4, 256, 256), BF),
+            dma((6,)),
             pltpu.VMEM((32, 16, 128), BF),
             pltpu.VMEM((32, 16, 128), BF),
             pltpu.VMEM((8, 2, 16, 128), BF),
@@ -280,12 +312,14 @@
             pltpu.VMEM((128, 512), F32),
             pltpu.VMEM((2, 64, 512), BF),
             pltpu.VMEM((2, 64, 512), BF),
-            dma((31,)), dma((31,)), dma((7,)), dma((7,)), dma((3,)), dma((3,)), dma((7,)), dma((7,)),
-            dma((3, 3)), dma((3, 3)), dma((7,)), dma((7,)), dma(()), dma(()),
+            dma((31,)), dma((31,)), dma((7,)), dma((8,)), dma((3,)), dma((3,)), dma((3, 7)), dma((3, 8)),
+            dma((3, 3)), dma((3, 3)), dma((7,)), dma((8,)), dma(()), dma(()),
         ],
-        compiler_params=pltpu.CompilerParams(collective_id=0, has_side_effects=True, vmem_limit_bytes=40 << 20),
+        compiler_params=pltpu.CompilerParams(collective_id=0, has_side_effects=True, vmem_limit_bytes=107 << 19),
         name="match",
     )(quarter_turns, plan, micrographs, templates, jnp.asarray(fwd), jnp.asarray(fwd_t))
+    scale = 1.0 / (SIDE * SIDE)
+    return raw[0:1] * scale, raw[1:2] * (scale / SEARCHED)
 
 
 def solution(mesh):

time: 58.4 us -> 47.7 us (0.82)
  Pallas kernels: 51.4 us -> 44.6 us
  local copies, waits for them, and re-layouts: 5.34 us -> 0.9 us
  other arithmetic: 0 us -> 0.72 us
    pallas_call x1, Pallas kernels: 51.4 us -> 44.6 us  [per_device(): pl.pallas_call(kernel, out_shape=jax.ShapeDtypeStruct((2, 64, SIDE), F32)...]
    unnamed x12 -> x4, local copies, waits for them, and re-layouts: 5.34 us -> 0.9 us
    mul x0 -> x1, other arithmetic: none -> 0.72 us  [per_device(): return (raw[0:1] * scale, raw[1:2] * (scale / SEARCHED))]
where the time goes in v2:
time: 47.7 us; the launch traced here: 47.6 us
  Pallas kernels  44.6 us (94%)
  between operations  1.32 us (3%)
  local copies, waits for them, and re-layouts  0.9 us (2%)
  other arithmetic  0.72 us (2%)
    pallas_call x1, Pallas kernels, per_device(): pl.pallas_call(kernel, out_shape=jax.ShapeDtypeStruct((2, 64, SIDE), F32)...  44.6 us

profile of v2, /device:TPU:1, one launch (start us, length us, event | category | flops | bytes accessed | tf_op | source)
XLA Modules:
  0.0 47.6 jit_solution(2744183466280191332)
XLA Ops:
  0.6 0.0 copy-start.1
  1.3 0.0 copy-done.1
  1.3 0.0 copy-start
  1.3 0.9 %copy-done = bf16[1,1,256,256]{3,2,1,0:T(8,128)(2,1)S(1)} copy-done((bf16[1,1,256,256]{3,2,1,0:T(8,128)(2,1)S(1)}, bf16[1,1,256,256]{3,2,1,0:T(8,128)(2,1)}, u32[]{:S(2)}) %copy-start) | copy-done | bytes 131096
  2.2 44.6 %match.1 = f32[2,64,512]{2,1,0:T(8,128)S(1)} custom-call(s32[1,1]{1,0:T(1,128)S(6)} %copy.8.quarter_in, s32[64]{0:T(128)S(1)} %copy-done.1, bf16[1,512,512]{2,1,0:T(8,128)(2,1)} %mic_in.1, bf16[1,1,256,256]{3,2,1,0:T(8,128)(2,1)S(1)} %copy-done, bf16[4,256,256]{2,1,0:T(8,128)(2,1)} %constant.8.clone.fwd_in, bf16[4,256,256]{2,1,0:T(8,128)(2,1)} %constant.9.clone.fwd_t_in), custom_call_target="tpu_custom_call" | custom-call | tf_op jit(solution)/shard_map/match/pallas_call | solution.py:289
  46.8 0.7 %slice_multiply_fusion = (f32[1,64,512]{2,1,0:T(8,128)}, f32[1,64,512]{2,1,0:T(8,128)}) fusion(f32[2,64,512]{2,1,0:T(8,128)S(1)} %match.1), kind=kLoop, calls=%fused_computation | loop fusion | flops 65536 | bytes 524288 | tf_op jit(solution)/shard_map/mul | solution.py:322
Async XLA Ops:
  0.6 0.7 %copy-start.1 = (s32[64]{0:T(128)S(1)}, s32[64]{0:T(128)}, u32[]{:S(2)}) copy-start(s32[64]{0:T(128)} %plan_in.1) | copy-start | bytes 772
  1.3 0.9 %copy-start = (bf16[1,1,256,256]{3,2,1,0:T(8,128)(2,1)S(1)}, bf16[1,1,256,256]{3,2,1,0:T(8,128)(2,1)}, u32[]{:S(2)}) copy-start(bf16[1,1,256,256]{3,2,1,0:T(8,128)(2,1)} %tmpl_in.1) | copy-start | bytes 393220

commit v3 on v2

--- a/solution.py
+++ b/solution.py
@@ -147,32 +147,45 @@
 def kernel(
     quarter_in, plan_in, mic_in, tmpl_in, fwd_in, fwd_t_in, out,
     quarter, plan, mic, tmpl, fwd, fwd_t, load, turned, got, line, tx, tz, spec, work, prod, left, best, total, give, take,
-    a_send, a_recv, y_send, y_recv, sx_send, sx_recv, sz_send, sz_recv, bx_send, bx_recv, bz_send, bz_recv, c_send, c_recv,
+    a_send, a_recv, y_send, y_recv, sx_send, sx_recv, sz_send, sz_recv, lz_send, lz_recv, bx_send, bx_recv, bz_send, bz_recv, c_send, c_recv,
 ):
     x, z, y, core = coords()
-
-    def hops(dx, dz):
-        return min(dx, 4 - dx) + min(dz, 8 - dz)
-
-    around = [(dx, dz) for dx in range(4) for dz in range(8) if (dx, dz) != (0, 0)]
-    around.sort(key=lambda step: -hops(*step))
-    plane = [(lax.rem(x + dx, 4), lax.rem(z + dz, 8)) for dx, dz in around]
-    x_peers = [device(lax.rem(x + d, 4), z, y, core) for d in (2, 1, 3)]
+    early = z < 4
+    late = z >= 4
+    x_ways = [lax.rem(x + d, 4) for d in (2, 1, 3)]
+    x_peers = [device(px, z, y, core) for px in x_ways]
     y_peers = [device(x, z, lax.rem(y + d, 8), core) for d in (4, 3, 5, 2, 6, 1, 7)]
-    z_others = [k + (z <= k).astype(jnp.int32) for k in range(7)]
-    z_peers = [device(x, other_z, y, core) for other_z in z_others]
+    part = jnp.where(early, z, 7 - z)
+    others = [k + (part <= k).astype(jnp.int32) for k in range(3)]
+    z_peers = [device(x, jnp.where(early, k, 7 - k), y, core) for k in others]
+    partner = device(x, 7 - z, y, core)
     other = device(x, z, y, 1 - core)
+    columns = x_ways + [x]
 
     barrier = pltpu.get_barrier_semaphore()
-    greeted = [device(px, pz, y, core) for px, pz in plane] + y_peers + [other]
+
+    def greet(target):
+        pl.semaphore_signal(barrier, inc=1, device_id=target, device_id_type=MESH)
+
+    @pl.when(early)
+    def _():
+        for px in columns:
+            for pz in (7, 6, 5, 4, 3, 2, 1, 0):
+
+                @pl.when((px != x) | (z != pz))
+                def _():
+                    greet(device(px, pz, y, core))
+
+        for target in y_peers:
+            greet(target)
+
+    greet(other)
     loads = [
         pltpu.make_async_copy(src, dst, load.at[i])
         for i, (src, dst) in enumerate(
             [(quarter_in, quarter), (tmpl_in, tmpl), (fwd_in, fwd), (mic_in, mic), (fwd_t_in, fwd_t), (plan_in, plan)]
         )
     ]
-    for target in greeted:
-        pl.semaphore_signal(barrier, inc=1, device_id=target, device_id_type=MESH)
     for copy in loads:
         copy.start()
     loads[0].wait()
@@ -181,77 +194,131 @@
     block = rotate(tmpl[0, 0], quarter[0, 0])
     for q in range(2):
         for h in range(2):
-            turned[pl.ds(16 * q + 8 * h, 8)] = block[128 * q : 128 * q + 128, 128 * h : 128 * h + 128].reshape(8, 16, 128)
-    pl.semaphore_wait(barrier, len(greeted))
+            chunks = block[128 * q : 128 * q + 128, 128 * h : 128 * h + 128].reshape(4, 2, 16, 128)
+            turned[pl.ds(8 * q + 4 * h, 4)] = chunks
+
+    @pl.when(early)
+    def _():
+        pl.semaphore_wait(barrier, 23)
+
+    @pl.when(late)
+    def _():
+        pl.semaphore_wait(barrier, 17)
 
     mine = x * 8 + z
-    sends = []
-    for i, (px, pz) in enumerate(plane):
-        copy = remote(turned.at[px * 8 + pz], got.at[mine], a_send.at[i], a_recv.at[i], device(px, pz, y, core))
-        copy.start()
-        sends.append(copy)
-    got[mine] = turned[mine]
+
+    def scatter(k, pz):
+        px = columns[k]
+        return remote(
+            turned.at[px * 4 + pz], got.at[mine], a_send.at[4 * k + pz], a_recv.at[mine], device(px, pz, y, core)
+        )
+
+    for k in range(4):
+        for pz in (3, 0, 2, 1):
+
+            @pl.when((z != pz) if k == 3 else (z >= 0))
+            def _():
+                scatter(k, pz).start()
+
     for copy in loads[2:]:
         copy.wait()
     tile_spectrum(mic, fwd, fwd_t, work, spec)
     inverse_rows(fwd_t, lax.div(y, 2), left)
-    for copy in sends:
-        copy.wait_recv()
-
-    owners = [plan[s] for s in range(2)]
-    for s in range(2):
-        line[y, s] = got[lax.div(owners[s], 2)]
-    for i, target in enumerate(y_peers):
-        copy = remote(line.at[y], line.at[y], y_send.at[i], y_recv.at[y], target)
-        copy.start()
-        sends.append(copy)
-
-    odd = [jnp.full((16, 128), lax.rem(owners[s], 2), jnp.int32) for s in range(2)]
-
-    def arrived(pair):
-        for low in range(2):
-            source = 2 * pair + low
-
-            @pl.when(source != y)
-            def _():
-                remote(line.at[source], line.at[source], y_send.at[0], y_recv.at[source], other).wait_recv()
-
-        return [jnp.where(odd[s] == 0, line[2 * pair, s], line[2 * pair + 1, s]) for s in range(2)]
-
-    own = lax.div(y, 2)
-    for s, tile in enumerate(arrived(own)):
-        tz[z, x, s] = tile
-    x_copies = [
-        remote(tz.at[z, x], tz.at[z, x], sx_send.at[i], sx_recv.at[i], target) for i, target in enumerate(x_peers)
-    ]
-    for copy in x_copies:
-        copy.start()
-    for p, step in enumerate((1, 3, 2)):
-        for s, tile in enumerate(arrived(lax.rem(own + step, 4))):
-            tx[x, p, z, s] = tile
-        for i, target in enumerate(z_peers):
-            copy = remote(tx.at[x, p, z], tx.at[x, p, z], sz_send.at[p, i], sz_recv.at[p, z], target)
-            copy.start()
-            sends.append(copy)
-    for copy in x_copies:
-        copy.wait_recv()
-    for i, target in enumerate(z_peers):
-        copy = remote(tz.at[z], tz.at[z], bz_send.at[i], bz_recv.at[z], target)
-        copy.start()
-        sends.append(copy)
-    last_x = []
+
+    mine_z = pl.ds(2 * part, 2)
+
+    def z_first(p, i):
+        ref = tx.at[x, p, mine_z]
+        return remote(ref, ref, sz_send.at[p, i], sz_recv.at[p, part], z_peers[i])
+
+    def z_first_from(p, k):
+        ref = tx.at[x, p, pl.ds(2 * k, 2)]
+        return remote(ref, ref, sz_send.at[p, 0], sz_recv.at[p, k], other)
+
+    def x_first(i):
+        ref = tz.at[mine_z, x]
+        return remote(ref, ref, sx_send.at[i], sx_recv.at[i], x_peers[i])
+
+    def z_last(i):
+        return remote(tz.at[mine_z], tz.at[mine_z], bz_send.at[i], bz_recv.at[part], z_peers[i])
+
+    def z_last_from(k):
+        ref = tz.at[pl.ds(2 * k, 2)]
+        return remote(ref, ref, bz_send.at[0], bz_recv.at[k], other)
+
+    def across(p):
+        ref = tz.at[mine_z, x] if p == 3 else tx.at[x, p, mine_z]
+        return remote(ref, ref, lz_send.at[p], lz_recv.at[p], partner)
+
+    def x_last(p, i):
+        return remote(tx.at[x, p], tx.at[x, p], bx_send.at[p, i], bx_recv.at[p, i], x_peers[i])
+
+    def to_y(i):
+        return remote(line.at[y], line.at[y], y_send.at[i], y_recv.at[y], y_peers[i])
+
+    @pl.when(early)
+    def _():
+        got[mine] = turned[x * 4 + z]
+        for k in range(4):
+            for pz in range(8):
+                source = columns[k] * 8 + pz
+
+                @pl.when((z != pz) if k == 3 else (z >= 0))
+                def _():
+                    remote(turned.at[0], got.at[source], a_send.at[0], a_recv.at[source], other).wait_recv()
+
+        owners = [plan[s] for s in range(2)]
+        for s in range(2):
+            line[y, s] = got[lax.div(owners[s], 2)]
+        for i in range(7):
+            to_y(i).start()
+        odd = [jnp.full((2, 16, 128), lax.rem(owners[s], 2), jnp.int32) for s in range(2)]
+
+        def arrived(pair):
+            for low in range(2):
+                source = 2 * pair + low
+
+                @pl.when(source != y)
+                def _():
+                    remote(line.at[source], line.at[source], y_send.at[0], y_recv.at[source], other).wait_recv()
+
+            return [jnp.where(odd[s] == 0, line[2 * pair, s], line[2 * pair + 1, s]) for s in range(2)]
+
+        own = lax.div(y, 2)
+        for s, tiles in enumerate(arrived(own)):
+            for b in range(2):
+                tz[2 * z + b, x, s] = tiles[b]
+        for i in range(3):
+            x_first(i).start()
+        across(3).start()
+        for p, pairs in enumerate(((1, 0, 1, 0), (3, 3, 3, 1), (2, 2, 0, 2))):
+            chosen = jnp.where(own < 2, jnp.where(own == 0, pairs[0], pairs[1]), jnp.where(own == 2, pairs[2], pairs[3]))
+            for s, tiles in enumerate(arrived(chosen)):
+                for b in range(2):
+                    tx[x, p, 2 * z + b, s] = tiles[b]
+            for i in range(3):
+                z_first(p, i).start()
+            across(p).start()
+
+    @pl.when(late)
+    def _():
+        across(3).wait_recv()
+        for i in range(3):
+            x_first(i).start()
+        for p in range(3):
+            across(p).wait_recv()
+            for i in range(3):
+                z_first(p, i).start()
+
+    for i in range(3):
+        x_first(i).wait_recv()
+    for i in range(3):
+        z_last(i).start()
     for p in range(3):
-        for i, source in enumerate(z_others):
-            remote(tx.at[x, p, source], tx.at[x, p, source], sz_send.at[p, i], sz_recv.at[p, source], other).wait_recv()
-        group = [
-            remote(tx.at[x, p], tx.at[x, p], bx_send.at[p, i], bx_recv.at[p, i], target)
-            for i, target in enumerate(x_peers)
-        ]
-        for copy in group:
-            copy.start()
-        last_x.append(group)
-        sends += group
-    sends += x_copies
+        for k in others:
+            z_first_from(p, k).wait_recv()
+        for i in range(3):
+            x_last(p, i).start()
 
     def from_x(p):
         return lambda q, h, s: tx[2 * q + h, p, :, s].reshape(128, 128)
@@ -259,15 +326,16 @@
     def from_z(q, h, s):
         return tz[:, 2 * q + h, s].reshape(128, 128)
 
-    for copy in last_x[0]:
-        copy.wait_recv()
+    for i in range(3):
+        x_last(0, i).wait_recv()
     pair_scores(from_x(0), fwd, fwd_t, spec, left, work, prod, best, total, True)
-    for i, source in enumerate(z_others):
-        remote(tz.at[source], tz.at[source], bz_send.at[i], bz_recv.at[source], other).wait_recv()
+
+    for k in others:
+        z_last_from(k).wait_recv()
     pair_scores(from_z, fwd, fwd_t, spec, left, work, prod, best, total, False)
     for p in range(1, 3):
-        for copy in last_x[p]:
-            copy.wait_recv()
+        for i in range(3):
+            x_last(p, i).wait_recv()
         pair_scores(from_x(p), fwd, fwd_t, spec, left, work, prod, best, total, False)
 
     theirs, ours = pl.ds((1 - core) * 64, 64), pl.ds(core * 64, 64)
@@ -279,8 +347,26 @@
     out[0] = jnp.maximum(best[ours, :], take[0].astype(F32))
     out[1] = total[ours, :] + take[1].astype(F32)
     swap.wait_send()
-    for copy in sends:
-        copy.wait_send()
+    for k in range(4):
+        for pz in range(4):
+
+            @pl.when((z != pz) if k == 3 else (z >= 0))
+            def _():
+                scatter(k, pz).wait_send()
+
+    for i in range(3):
+        x_first(i).wait_send()
+        z_last(i).wait_send()
+        for p in range(3):
+            z_first(p, i).wait_send()
+            x_last(p, i).wait_send()
+
+    @pl.when(early)
+    def _():
+        for i in range(7):
+            to_y(i).wait_send()
+        for p in range(4):
+            across(p).wait_send()
 
 
 def per_device(micrographs, templates, quarter_turns, plan):
@@ -299,9 +385,9 @@
             pltpu.VMEM((4, 256, 256), BF),
             pltpu.VMEM((4, 256, 256), BF),
             dma((6,)),
-            pltpu.VMEM((32, 16, 128), BF),
-            pltpu.VMEM((32, 16, 128), BF),
-            pltpu.VMEM((8, 2, 16, 128), BF),
+            pltpu.VMEM((16, 2, 16, 128), BF),
+            pltpu.VMEM((32, 2, 16, 128), BF),
+            pltpu.VMEM((8, 2, 2, 16, 128), BF),
             pltpu.VMEM((4, 3, 8, 2, 16, 128), BF),
             pltpu.VMEM((8, 4, 2, 16, 128), BF),
             pltpu.VMEM((4, 512, 256), BF),
@@ -312,8 +398,8 @@
             pltpu.VMEM((128, 512), F32),
             pltpu.VMEM((2, 64, 512), BF),
             pltpu.VMEM((2, 64, 512), BF),
-            dma((31,)), dma((31,)), dma((7,)), dma((8,)), dma((3,)), dma((3,)), dma((3, 7)), dma((3, 8)),
-            dma((3, 3)), dma((3, 3)), dma((7,)), dma((8,)), dma(()), dma(()),
+            dma((16,)), dma((32,)), dma((7,)), dma((8,)), dma((3,)), dma((3,)), dma((3, 3)), dma((3, 4)), dma((4,)), dma((4,)),
+            dma((3, 3)), dma((3, 3)), dma((3,)), dma((4,)), dma(()), dma(()),
         ],
         compiler_params=pltpu.CompilerParams(collective_id=0, has_side_effects=True, vmem_limit_bytes=107 << 19),
         name="match",

time: 47.7 us -> 46.9 us (0.983)
  Pallas kernels: 44.6 us -> 43.8 us
    pallas_call x1, Pallas kernels: 44.6 us -> 43.8 us  [per_device(): pl.pallas_call(kernel, out_shape=jax.ShapeDtypeStruct((2, 64, SIDE), F32)...]
where the time goes in v3:
time: 46.9 us; the launch traced here: 46.8 us
  Pallas kernels  43.8 us (93%)
  between operations  1.32 us (3%)
  local copies, waits for them, and re-layouts  0.9 us (2%)
  other arithmetic  0.72 us (2%)
    pallas_call x1, Pallas kernels, per_device(): pl.pallas_call(kernel, out_shape=jax.ShapeDtypeStruct((2, 64, SIDE), F32)...  43.8 us

profile of v3, /device:TPU:1, one launch (start us, length us, event | category | flops | bytes accessed | tf_op | source)
XLA Modules:
  0.0 46.8 jit_solution(4663705508930795655)
XLA Ops:
  0.6 0.0 copy-start.1
  1.3 0.0 copy-done.1
  1.3 0.0 copy-start
  1.3 0.9 %copy-done = bf16[1,1,256,256]{3,2,1,0:T(8,128)(2,1)S(1)} copy-done((bf16[1,1,256,256]{3,2,1,0:T(8,128)(2,1)S(1)}, bf16[1,1,256,256]{3,2,1,0:T(8,128)(2,1)}, u32[]{:S(2)}) %copy-start) | copy-done | bytes 131096
  2.2 43.8 %match.1 = f32[2,64,512]{2,1,0:T(8,128)S(1)} custom-call(s32[1,1]{1,0:T(1,128)S(6)} %copy.8.quarter_in, s32[64]{0:T(128)S(1)} %copy-done.1, bf16[1,512,512]{2,1,0:T(8,128)(2,1)} %mic_in.1, bf16[1,1,256,256]{3,2,1,0:T(8,128)(2,1)S(1)} %copy-done, bf16[4,256,256]{2,1,0:T(8,128)(2,1)} %constant.8.clone.fwd_in, bf16[4,256,256]{2,1,0:T(8,128)(2,1)} %constant.9.clone.fwd_t_in), custom_call_target="tpu_custom_call" | custom-call | tf_op jit(solution)/shard_map/match/pallas_call | solution.py:375
  46.0 0.7 %slice_multiply_fusion = (f32[1,64,512]{2,1,0:T(8,128)}, f32[1,64,512]{2,1,0:T(8,128)}) fusion(f32[2,64,512]{2,1,0:T(8,128)S(1)} %match.1), kind=kLoop, calls=%fused_computation | loop fusion | flops 65536 | bytes 524288 | tf_op jit(solution)/shard_map/mul | solution.py:408
Async XLA Ops:
  0.6 0.7 %copy-start.1 = (s32[64]{0:T(128)S(1)}, s32[64]{0:T(128)}, u32[]{:S(2)}) copy-start(s32[64]{0:T(128)} %plan_in.1) | copy-start | bytes 772
  1.3 0.9 %copy-start = (bf16[1,1,256,256]{3,2,1,0:T(8,128)(2,1)S(1)}, bf16[1,1,256,256]{3,2,1,0:T(8,128)(2,1)}, u32[]{:S(2)}) copy-start(bf16[1,1,256,256]{3,2,1,0:T(8,128)(2,1)} %tmpl_in.1) | copy-start | bytes 393220

commit v4 on v3

--- a/solution.py
+++ b/solution.py
@@ -101,11 +101,11 @@
 
 
 def pair_scores(block, fwd, fwd_t, spec, left, work, prod, best, total, first):
-    a0, a1 = [jnp.concatenate([block(q, 0, 0), block(q, 1, 0)], axis=1).astype(F32) for q in range(2)]
-    b0, b1 = [jnp.concatenate([block(q, 0, 1), block(q, 1, 1)], axis=1).astype(F32) for q in range(2)]
+    a0, a1 = [jnp.concatenate([block(q, 0, 0), block(q, 1, 0)], axis=1) for q in range(2)]
+    b0, b1 = [jnp.concatenate([block(q, 0, 1), block(q, 1, 1)], axis=1) for q in range(2)]
     stacked = [(a0 + a1, b0 + b1), (a0 + b1, b0 - a1), (a0 - a1, b0 - b1), (a0 - b1, b0 + a1)]
     for r1 in range(4):
-        out = dot(fwd[r1], jnp.concatenate(stacked[r1], axis=0).astype(BF))
+        out = dot(fwd[r1], jnp.concatenate(stacked[r1], axis=0))
         re0, re1, im0, im1 = out[:128, :128], out[:128, 128:], out[128:, :128], out[128:, 128:]
         rows = pl.ds(128 * r1, 128)
         pairs = [(re0 + re1, im0 + im1), (re0 + im1, im0 - re1), (re0 - re1, im0 - im1), (re0 - im1, im0 + re1)]
@@ -114,10 +114,10 @@
             work[r2, rows, 128:] = p_im.astype(BF)
     for r2 in range(4):
         found = dot(work[r2], fwd_t[r2])
-        t_re, t_im = found[:, :128].astype(BF).astype(F32), found[:, 128:].astype(BF).astype(F32)
-        x_re, x_im = spec[r2, :, :128].astype(F32), spec[r2, :, 128:].astype(F32)
-        p_re = (x_re * t_re + x_im * t_im).astype(BF)
-        p_im = (x_im * t_re - x_re * t_im).astype(BF)
+        t_re, t_im = found[:, :128].astype(BF), found[:, 128:].astype(BF)
+        x_re, x_im = spec[r2, :, :128], spec[r2, :, 128:]
+        p_re = x_re * t_re + x_im * t_im
+        p_im = x_im * t_re - x_re * t_im
         lanes = pl.ds(128 * r2, 128)
         for r1 in range(4):
             prod[pl.ds(256 * r1, 128), lanes] = p_re[128 * r1 : 128 * r1 + 128]
@@ -372,6 +372,7 @@
 def per_device(micrographs, templates, quarter_turns, plan):
     fwd, fwd_t = radix_tables()
     dma = pltpu.SemaphoreType.DMA
+    operands = (quarter_turns, plan, micrographs, templates, jnp.asarray(fwd), jnp.asarray(fwd_t))
     raw = pl.pallas_call(
         kernel,
         out_shape=jax.ShapeDtypeStruct((2, 64, SIDE), F32),
@@ -401,9 +402,9 @@
             dma((16,)), dma((32,)), dma((7,)), dma((8,)), dma((3,)), dma((3,)), dma((3, 3)), dma((3, 4)), dma((4,)), dma((4,)),
             dma((3, 3)), dma((3, 3)), dma((3,)), dma((4,)), dma(()), dma(()),
         ],
-        compiler_params=pltpu.CompilerParams(collective_id=0, has_side_effects=True, vmem_limit_bytes=107 << 19),
+        compiler_params=pltpu.CompilerParams(collective_id=0, has_side_effects=True, vmem_limit_bytes=40 << 20),
         name="match",
-    )(quarter_turns, plan, micrographs, templates, jnp.asarray(fwd), jnp.asarray(fwd_t))
+    )(operands[0], *[pltpu.with_memory_space_constraint(a, pltpu.HBM) for a in operands[1:]])
     scale = 1.0 / (SIDE * SIDE)
     return raw[0:1] * scale, raw[1:2] * (scale / SEARCHED)
 

time: 46.9 us -> 45.7 us (0.974)
  local copies, waits for them, and re-layouts: 0.9 us -> 0 us
    unnamed x4 -> x0, local copies, waits for them, and re-layouts: 0.9 us -> none
where the time goes in v4:
time: 45.7 us; the launch traced here: 45.5 us
  Pallas kernels  43.5 us (95%)
  between operations  1.28 us (3%)
  other arithmetic  0.72 us (2%)
    pallas_call x1, Pallas kernels, per_device(): pl.pallas_call(kernel, out_shape=jax.ShapeDtypeStruct((2, 64, SIDE), F32)...  43.5 us

profile of v4, /device:TPU:1, one launch (start us, length us, event | category | flops | bytes accessed | tf_op | source)
XLA Modules:
  0.0 45.5 jit_solution(10854459601450475223)
XLA Ops:
  1.3 43.5 %match.1 = f32[2,64,512]{2,1,0:T(8,128)S(1)} custom-call(s32[1,1]{1,0:T(1,128)S(6)} %copy.8.quarter_in, s32[64]{0:T(128)} %plan_in.1, bf16[1,512,512]{2,1,0:T(8,128)(2,1)} %mic_in.1, bf16[1,1,256,256]{3,2,1,0:T(8,128)(2,1)} %tmpl_in.1, bf16[4,256,256]{2,1,0:T(8,128)(2,1)} %constant.8.clone.fwd_in, bf16[4,256,256]{2,1,0:T(8,128)(2,1)} %constant.9.clone.fwd_t_in), custom_call_target="tpu_custom_call" | custom-call | tf_op jit(solution)/shard_map/match/pallas_call | solution.py:376
  44.8 0.7 %slice_multiply_fusion = (f32[1,64,512]{2,1,0:T(8,128)}, f32[1,64,512]{2,1,0:T(8,128)}) fusion(f32[2,64,512]{2,1,0:T(8,128)S(1)} %match.1), kind=kLoop, calls=%fused_computation | loop fusion | flops 65536 | bytes 524288 | tf_op jit(solution)/shard_map/mul | solution.py:409

commit v5 on v4

--- a/solution.py
+++ b/solution.py
@@ -105,13 +105,13 @@
     b0, b1 = [jnp.concatenate([block(q, 0, 1), block(q, 1, 1)], axis=1) for q in range(2)]
     stacked = [(a0 + a1, b0 + b1), (a0 + b1, b0 - a1), (a0 - a1, b0 - b1), (a0 - b1, b0 + a1)]
     for r1 in range(4):
-        out = dot(fwd[r1], jnp.concatenate(stacked[r1], axis=0))
+        out = dot(fwd[r1], jnp.concatenate(stacked[r1], axis=0)).astype(BF)
         re0, re1, im0, im1 = out[:128, :128], out[:128, 128:], out[128:, :128], out[128:, 128:]
         rows = pl.ds(128 * r1, 128)
         pairs = [(re0 + re1, im0 + im1), (re0 + im1, im0 - re1), (re0 - re1, im0 - im1), (re0 - im1, im0 + re1)]
         for r2, (p_re, p_im) in enumerate(pairs):
-            work[r2, rows, :128] = p_re.astype(BF)
-            work[r2, rows, 128:] = p_im.astype(BF)
+            work[r2, rows, :128] = p_re
+            work[r2, rows, 128:] = p_im
     for r2 in range(4):
         found = dot(work[r2], fwd_t[r2])
         t_re, t_im = found[:, :128].astype(BF), found[:, 128:].astype(BF)
@@ -326,13 +326,13 @@
     def from_z(q, h, s):
         return tz[:, 2 * q + h, s].reshape(128, 128)
 
+    for k in others:
+        z_last_from(k).wait_recv()
+    pair_scores(from_z, fwd, fwd_t, spec, left, work, prod, best, total, True)
     for i in range(3):
         x_last(0, i).wait_recv()
-    pair_scores(from_x(0), fwd, fwd_t, spec, left, work, prod, best, total, True)
-
-    for k in others:
-        z_last_from(k).wait_recv()
-    pair_scores(from_z, fwd, fwd_t, spec, left, work, prod, best, total, False)
+    pair_scores(from_x(0), fwd, fwd_t, spec, left, work, prod, best, total, False)
+
     for p in range(1, 3):
         for i in range(3):
             x_last(p, i).wait_recv()

time: 45.7 us -> 45.6 us (level)
  no operation moved by 1% of the time
where the time goes in v5:
time: 45.6 us; the launch traced here: 45.5 us
  Pallas kernels  43.5 us (95%)
  between operations  1.28 us (3%)
  other arithmetic  0.72 us (2%)
    pallas_call x1, Pallas kernels, per_device(): pl.pallas_call(kernel, out_shape=jax.ShapeDtypeStruct((2, 64, SIDE), F32)...  43.5 us

profile of v5, /device:TPU:1, one launch (start us, length us, event | category | flops | bytes accessed | tf_op | source)
XLA Modules:
  0.0 45.5 jit_solution(3757401749391323483)
XLA Ops:
  1.3 43.5 %match.1 = f32[2,64,512]{2,1,0:T(8,128)S(1)} custom-call(s32[1,1]{1,0:T(1,128)S(6)} %copy.8.quarter_in, s32[64]{0:T(128)} %plan_in.1, bf16[1,512,512]{2,1,0:T(8,128)(2,1)} %mic_in.1, bf16[1,1,256,256]{3,2,1,0:T(8,128)(2,1)} %tmpl_in.1, bf16[4,256,256]{2,1,0:T(8,128)(2,1)} %constant.8.clone.fwd_in, bf16[4,256,256]{2,1,0:T(8,128)(2,1)} %constant.9.clone.fwd_t_in), custom_call_target="tpu_custom_call" | custom-call | tf_op jit(solution)/shard_map/match/pallas_call | solution.py:376
  44.8 0.7 %slice_multiply_fusion = (f32[1,64,512]{2,1,0:T(8,128)}, f32[1,64,512]{2,1,0:T(8,128)}) fusion(f32[2,64,512]{2,1,0:T(8,128)S(1)} %match.1), kind=kLoop, calls=%fused_computation | loop fusion | flops 65536 | bytes 524288 | tf_op jit(solution)/shard_map/mul | solution.py:409

commit v6 on v5

--- a/solution.py
+++ b/solution.py
@@ -100,7 +100,7 @@
         left[128:, 256 * r : 256 * r + 128] = new_s.astype(BF)
 
 
-def pair_scores(block, fwd, fwd_t, spec, left, work, prod, best, total, first):
+def pair_scores(block, fwd, fwd_t, spec, left, work, prod, best, total, first, done=None):
     a0, a1 = [jnp.concatenate([block(q, 0, 0), block(q, 1, 0)], axis=1) for q in range(2)]
     b0, b1 = [jnp.concatenate([block(q, 0, 1), block(q, 1, 1)], axis=1) for q in range(2)]
     stacked = [(a0 + a1, b0 + b1), (a0 + b1, b0 - a1), (a0 - a1, b0 - b1), (a0 - b1, b0 + a1)]
@@ -142,6 +142,8 @@
         else:
             best[:, lanes] = jnp.maximum(best[:, lanes], top)
             total[:, lanes] = total[:, lanes] + both
+        if done is not None:
+            done(q)
 
 
 def kernel(
@@ -156,7 +158,9 @@
     x_peers = [device(px, z, y, core) for px in x_ways]
     y_peers = [device(x, z, lax.rem(y + d, 8), core) for d in (4, 3, 5, 2, 6, 1, 7)]
     part = jnp.where(early, z, 7 - z)
-    others = [k + (part <= k).astype(jnp.int32) for k in range(3)]
+    mirrored = jnp.where(early, part, 3 - part)
+    others = [k + (mirrored <= k).astype(jnp.int32) for k in range(3)]
+    others = [jnp.where(early, k, 3 - k) for k in others]
     z_peers = [device(x, jnp.where(early, k, 7 - k), y, core) for k in others]
     partner = device(x, 7 - z, y, core)
     other = device(x, z, y, 1 - core)
@@ -288,17 +292,17 @@
         for s, tiles in enumerate(arrived(own)):
             for b in range(2):
                 tz[2 * z + b, x, s] = tiles[b]
+        across(3).start()
         for i in range(3):
             x_first(i).start()
-        across(3).start()
         for p, pairs in enumerate(((1, 0, 1, 0), (3, 3, 3, 1), (2, 2, 0, 2))):
             chosen = jnp.where(own < 2, jnp.where(own == 0, pairs[0], pairs[1]), jnp.where(own == 2, pairs[2], pairs[3]))
             for s, tiles in enumerate(arrived(chosen)):
                 for b in range(2):
                     tx[x, p, 2 * z + b, s] = tiles[b]
+            across(p).start()
             for i in range(3):
                 z_first(p, i).start()
-            across(p).start()
 
     @pl.when(late)
     def _():
@@ -333,20 +337,29 @@
         x_last(0, i).wait_recv()
     pair_scores(from_x(0), fwd, fwd_t, spec, left, work, prod, best, total, False)
 
+    theirs, ours = pl.ds((1 - core) * 64, 64), pl.ds(core * 64, 64)
+
+    def swap(q):
+        return remote(give.at[q], take.at[q], c_send.at[q], c_recv.at[q], other)
+
+    def hand_over(q):
+        lanes = pl.ds(128 * q, 128)
+        give[q, 0] = best[theirs, lanes].astype(BF)
+        give[q, 1] = total[theirs, lanes].astype(BF)
+        swap(q).start()
+
     for p in range(1, 3):
         for i in range(3):
             x_last(p, i).wait_recv()
-        pair_scores(from_x(p), fwd, fwd_t, spec, left, work, prod, best, total, False)
-
-    theirs, ours = pl.ds((1 - core) * 64, 64), pl.ds(core * 64, 64)
-    give[0] = best[theirs, :].astype(BF)
-    give[1] = total[theirs, :].astype(BF)
-    swap = remote(give, take, c_send, c_recv, other)
-    swap.start()
-    swap.wait_recv()
-    out[0] = jnp.maximum(best[ours, :], take[0].astype(F32))
-    out[1] = total[ours, :] + take[1].astype(F32)
-    swap.wait_send()
+        done = hand_over if p == 2 else None
+        pair_scores(from_x(p), fwd, fwd_t, spec, left, work, prod, best, total, False, done)
+    for q in range(4):
+        lanes = pl.ds(128 * q, 128)
+        swap(q).wait_recv()
+        out[0, :, lanes] = jnp.maximum(best[ours, lanes], take[q, 0].astype(F32))
+        out[1, :, lanes] = total[ours, lanes] + take[q, 1].astype(F32)
+    for q in range(4):
+        swap(q).wait_send()
     for k in range(4):
         for pz in range(4):
 
@@ -397,10 +410,10 @@
             pltpu.VMEM((256, 1024), BF),
             pltpu.VMEM((128, 512), F32),
             pltpu.VMEM((128, 512), F32),
-            pltpu.VMEM((2, 64, 512), BF),
-            pltpu.VMEM((2, 64, 512), BF),
+            pltpu.VMEM((4, 2, 64, 128), BF),
+            pltpu.VMEM((4, 2, 64, 128), BF),
             dma((16,)), dma((32,)), dma((7,)), dma((8,)), dma((3,)), dma((3,)), dma((3, 3)), dma((3, 4)), dma((4,)), dma((4,)),
-            dma((3, 3)), dma((3, 3)), dma((3,)), dma((4,)), dma(()), dma(()),
+            dma((3, 3)), dma((3, 3)), dma((3,)), dma((4,)), dma((4,)), dma((4,)),
         ],
         compiler_params=pltpu.CompilerParams(collective_id=0, has_side_effects=True, vmem_limit_bytes=40 << 20),
         name="match",

time: 45.6 us -> 45.7 us (level)
  no operation moved by 1% of the time
where the time goes in v6:
time: 45.7 us; the launch traced here: 45.5 us
  Pallas kernels  43.5 us (95%)
  between operations  1.28 us (3%)
  other arithmetic  0.72 us (2%)
    pallas_call x1, Pallas kernels, per_device(): pl.pallas_call(kernel, out_shape=jax.ShapeDtypeStruct((2, 64, SIDE), F32)...  43.5 us

profile of v6, /device:TPU:1, one launch (start us, length us, event | category | flops | bytes accessed | tf_op | source)
XLA Modules:
  0.0 45.5 jit_solution(3842894326210036087)
XLA Ops:
  1.3 43.5 %match.1 = f32[2,64,512]{2,1,0:T(8,128)S(1)} custom-call(s32[1,1]{1,0:T(1,128)S(6)} %copy.8.quarter_in, s32[64]{0:T(128)} %plan_in.1, bf16[1,512,512]{2,1,0:T(8,128)(2,1)} %mic_in.1, bf16[1,1,256,256]{3,2,1,0:T(8,128)(2,1)} %tmpl_in.1, bf16[4,256,256]{2,1,0:T(8,128)(2,1)} %constant.8.clone.fwd_in, bf16[4,256,256]{2,1,0:T(8,128)(2,1)} %constant.9.clone.fwd_t_in), custom_call_target="tpu_custom_call" | custom-call | tf_op jit(solution)/shard_map/match/pallas_call | solution.py:389
  44.8 0.7 %slice_multiply_fusion = (f32[1,64,512]{2,1,0:T(8,128)}, f32[1,64,512]{2,1,0:T(8,128)}) fusion(f32[2,64,512]{2,1,0:T(8,128)S(1)} %match.1), kind=kLoop, calls=%fused_computation | loop fusion | flops 65536 | bytes 524288 | tf_op jit(solution)/shard_map/mul | solution.py:422

commit v7 on v5

--- a/solution.py
+++ b/solution.py
@@ -170,7 +170,7 @@
     @pl.when(early)
     def _():
         for px in columns:
-            for pz in (7, 6, 5, 4, 3, 2, 1, 0):
+            for pz in range(4):
 
                 @pl.when((px != x) | (z != pz))
                 def _():
@@ -178,6 +178,9 @@
 
         for target in y_peers:
             greet(target)
+        for px in columns:
+            for pz in range(4, 8):
+                greet(device(px, pz, y, core))
 
     greet(other)
     loads = [

time: 45.6 us -> 45.8 us (level)
  no operation moved by 1% of the time
where the time goes in v7:
time: 45.8 us; the launch traced here: 45.7 us
  Pallas kernels  43.7 us (95%)
  between operations  1.28 us (3%)
  other arithmetic  0.72 us (2%)
    pallas_call x1, Pallas kernels, per_device(): pl.pallas_call(kernel, out_shape=jax.ShapeDtypeStruct((2, 64, SIDE), F32)...  43.7 us

profile of v7, /device:TPU:1, one launch (start us, length us, event | category | flops | bytes accessed | tf_op | source)
XLA Modules:
  0.0 45.7 jit_solution(4316243550420480773)
XLA Ops:
  1.3 43.7 %match.1 = f32[2,64,512]{2,1,0:T(8,128)S(1)} custom-call(s32[1,1]{1,0:T(1,128)S(6)} %copy.8.quarter_in, s32[64]{0:T(128)} %plan_in.1, bf16[1,512,512]{2,1,0:T(8,128)(2,1)} %mic_in.1, bf16[1,1,256,256]{3,2,1,0:T(8,128)(2,1)} %tmpl_in.1, bf16[4,256,256]{2,1,0:T(8,128)(2,1)} %constant.8.clone.fwd_in, bf16[4,256,256]{2,1,0:T(8,128)(2,1)} %constant.9.clone.fwd_t_in), custom_call_target="tpu_custom_call" | custom-call | tf_op jit(solution)/shard_map/match/pallas_call | solution.py:379
  45.0 0.7 %slice_multiply_fusion = (f32[1,64,512]{2,1,0:T(8,128)}, f32[1,64,512]{2,1,0:T(8,128)}) fusion(f32[2,64,512]{2,1,0:T(8,128)S(1)} %match.1), kind=kLoop, calls=%fused_computation | loop fusion | flops 65536 | bytes 524288 | tf_op jit(solution)/shard_map/mul | solution.py:412
